TPU v7x, 256 devices: a whole 4x4x8 slice. The times are simulated.
256 devices in a mesh: subj: 16 (over y, x), slab: 16 (over z, core).
Axes of the slice: x: 4, y: 4, z: 8, core: 2. Of those that a mesh axis runs over, the one named last changes fastest.
Arguments:
- template: float32 [8192, 128], P('slab'), may hold values from -6 to 6
- images: float32 [16, 8192, 128], P('subj', 'slab'), may hold values from -6 to 6
- velocity: float32 [16, 3, 8192, 128], P('subj', None, 'slab'), may hold values from -6 to 6
- stiffness: float32 [8192, 128], P('slab'), may hold values from 0.1 to 1
- send_rows: int32 [16, 16, 16, 32], P('subj', 'slab'), may hold values from 0 to 511, as said below
- ref_slot: int32 [16, 8192, 8], P('subj', 'slab'), may hold values from 0 to 511, as said below
- columns: int32 [16, 8192, 8, 128], P('subj', 'slab'), may hold values from 0 to 127, as said below
- weights: bfloat16 [16, 8192, 8, 128], P('subj', 'slab'), may hold values from 0 to 0.25
Outputs:
- template_out: float32 [8192, 128], P('slab')
- velocity_out: float32 [16, 3, 8192, 128], P('subj', None, 'slab')
Inputs may be any that keep to these rules, and one draw needn't show every extreme that they name: `send_rows`: local rows of the owner slab. `ref_slot`: for each subject and each owner k and destination slab j, the referenced c lie below a count of that pair between 16 and 32; for each subject one destination slab has the count 32 from every owner. columns[s, g, b, x] differs from x by at most 2.
All inputs are finite; a program needn't handle non-finite values.
Results may differ from a plain program's by a relative error of at most 0.0003.
Values sent between devices are 32-bit elements; how exact they have to be, the bound alone decides.
A program may use at most 64 MiB of HBM per device.

v0:
```python
import jax
import jax.numpy as jnp
from jax import lax
from jax.sharding import PartitionSpec as P

YR = 256
SMOOTH = 2
force_step = 1.0
diffusion_dt = 0.16
template_rate = 2.0


def extended(cells, sides, width):
    for axis, dim in sides:
        count = lax.axis_size(axis)
        ends = count - 1
        head = lax.slice_in_dim(cells, 0, width, axis=dim)
        tail = lax.slice_in_dim(cells, cells.shape[dim] - width, cells.shape[dim], axis=dim)
        cells = jnp.concatenate(
            [
                lax.ppermute(tail, axis, [(i, (i + 1) % count) for i in range(ends)]),
                cells,
                lax.ppermute(head, axis, [((i + 1) % count, i) for i in range(ends)]),
            ],
            axis=dim,
        )
    return cells


def smooth_step(field_padded, coef_padded):
    center = field_padded[:, 1:-1]
    coef_center = coef_padded[1:-1]
    field_yx = jnp.pad(center, ((0, 0), (0, 0), (1, 1), (1, 1)))
    coef_yx = jnp.pad(coef_center, ((0, 0), (1, 1), (1, 1)))
    pairs = [
        (field_padded[:, 2:], coef_padded[2:]),
        (field_padded[:, :-2], coef_padded[:-2]),
        (field_yx[:, :, 2:, 1:-1], coef_yx[:, 2:, 1:-1]),
        (field_yx[:, :, :-2, 1:-1], coef_yx[:, :-2, 1:-1]),
        (field_yx[:, :, 1:-1, 2:], coef_yx[:, 1:-1, 2:]),
        (field_yx[:, :, 1:-1, :-2], coef_yx[:, 1:-1, :-2]),
    ]
    summed = jnp.zeros(center.shape, jnp.float32)
    for neighbour, coef_near in pairs:
        face_coef = 0.5 * (coef_center + coef_near)
        summed = summed + face_coef[None] * (neighbour - center)
    return center + diffusion_dt * summed


def read_ahead(values, offset):
    if offset > 0:
        return jnp.concatenate(
            [values[..., offset:], jnp.zeros(values.shape[:-1] + (offset,), values.dtype)], axis=-1
        )
    if offset < 0:
        return jnp.concatenate(
            [jnp.zeros(values.shape[:-1] + (-offset,), values.dtype), values[..., :offset]], axis=-1
        )
    return values


def per_device(template, images, velocity, stiffness, send_rows, ref_slot, columns, weights):
    slabs = lax.axis_size("slab")
    subjects = lax.axis_size("subj")
    capacity = send_rows.shape[3]
    rows = template.shape[0]
    width = template.shape[1]
    planes = rows // YR
    send_one = send_rows[0, 0]
    sending = template[send_one]
    received = lax.all_to_all(sending, "slab", split_axis=0, concat_axis=0, tiled=True)
    flat_rows = received.reshape(slabs * capacity, width)
    slot_one = ref_slot[0]
    offset_one = columns[0] - jnp.arange(width, dtype=jnp.int32)
    picked = flat_rows[slot_one]
    weight_f = weights[0].astype(jnp.float32)
    values = jnp.zeros(picked.shape, jnp.float32)
    for offset in range(-2, 3):
        values = values + jnp.where(offset_one == offset, read_ahead(picked, offset), 0.0)
    warped = jnp.sum(weight_f * values, axis=1)
    mismatch = warped - images[0]
    contrib = weight_f * mismatch[:, None, :]
    placed = jnp.zeros(contrib.shape, jnp.float32)
    for offset in range(-2, 3):
        placed = placed + read_ahead(jnp.where(offset_one == offset, contrib, 0.0), -offset)
    slot_grad = (
        jnp.zeros((slabs * capacity, width), jnp.float32)
        .at[slot_one.reshape(-1)]
        .add(placed.reshape(-1, width))
    )
    slot_grad = slot_grad.reshape(slabs, capacity, width)
    returned = lax.all_to_all(slot_grad, "slab", split_axis=0, concat_axis=0, tiled=True)
    row_grad = (
        jnp.zeros((rows, width), jnp.float32)
        .at[send_one.reshape(-1)]
        .add(returned.reshape(-1, width))
    )
    summed = lax.psum(row_grad, "subj")
    template_out = template - template_rate * summed / subjects
    warped_grid = warped.reshape(planes, YR, width)
    warped_padded = extended(warped_grid, (("slab", 0),), 1)
    warped_yx = jnp.pad(warped_grid, ((0, 0), (1, 1), (1, 1)))
    along_x = 0.5 * (warped_yx[:, 1:-1, 2:] - warped_yx[:, 1:-1, :-2])
    along_y = 0.5 * (warped_yx[:, 2:, 1:-1] - warped_yx[:, :-2, 1:-1])
    along_z = 0.5 * (warped_padded[2:] - warped_padded[:-2])
    slopes = jnp.stack([along_x, along_y, along_z])
    field = (
        velocity[0].reshape(3, planes, YR, width)
        - force_step * mismatch.reshape(planes, YR, width)[None] * slopes
    )
    coef_grid = stiffness.reshape(planes, YR, width)
    coef_padded = extended(coef_grid, (("slab", 0),), 1)
    for repeat in range(SMOOTH):
        field_padded = extended(field, (("slab", 1),), 1)
        field = smooth_step(field_padded, coef_padded)
    velocity_out = field.reshape(3, rows, width)[None]
    return (template_out, velocity_out)


def solution(mesh):
    return jax.shard_map(
        per_device,
        mesh=mesh,
        in_specs=(
            P("slab", None),
            P("subj", "slab", None),
            P("subj", None, "slab", None),
            P("slab", None),
            P("subj", "slab", None, None),
            P("subj", "slab", None),
            P("subj", "slab", None, None),
            P("subj", "slab", None, None),
        ),
        out_specs=(P("slab", None), P("subj", None, "slab", None)),
        check_vma=False,
    )
```

profile of v0, /device:TPU:2, one launch (start us, length us, event | category | flops | bytes accessed | tf_op | source)
XLA Modules:
  0.0 206.6 jit_solution(10799320863399200082)
XLA Ops:
  7.2 0.0 copy-start.5
  7.2 0.0 copy-start.8
  7.2 0.7 compare_select_fusion.2
  7.9 0.1 reshape.168
  8.0 2.6 %gather_fusion = f32[512,128]{1,0:T(8,128)} fusion(f32[512,128]{1,0:T(8,128)} %param.8, s32[1024]{0:T(1024)S(1)} %pad_clamp_fusion), kind=kCustom, calls=%fused_computation | custom fusion | bytes 526336 | tf_op jit(solution)/shard_map/gather | solution.py:70
  10.6 8.6 %all-to-all-start = ((f32[16,32,128]{2,1,0:T(8,128)}), f32[16,32,128]{2,1,0:T(8,128)S(1)}, u32[]{:S(2)}, u32[]{:S(2)}) async-start(f32[16,32,128]{2,1,0:T(8,128)} %bitcast.6), calls=%async_computation | async-start | bytes 524288 | tf_op jit(solution)/shard_map/all_to_all | solution.py:71
  19.2 0.7 slice_bitcast_fusion.3
  19.9 1.3 collective-permute-start.2
  21.2 3.7 %collective-permute-start.4 = (f32[1,256,128]{2,1,0:T(8,128)}, f32[1,256,128]{2,1,0:T(8,128)}, u32[]{:S(2)}, u32[]{:S(2)}) collective-permute-start(f32[1,256,128]{2,1,0:T(8,128)} %get-tuple-element.27), channel_id=1, source_target_pairs={{0,1},{1,2},{2,3},{3,4},{4,5},{5,6},{6,7},{7,8},{8,9},{9,10},{10,1... | collective-permute-start | bytes 393224 | tf_op jit(solution)/shard_map/ppermute | solution.py:21
  24.9 0.1 copy.10
  25.0 0.2 reshape_squeeze.10
  25.3 0.7 reshape_squeeze.9
  25.9 0.1 copy.11
  26.1 0.2 reshape.176
  26.2 4.1 %all-to-all-done = f32[16,32,128]{2,1,0:T(8,128)S(1)} async-done(((f32[16,32,128]{2,1,0:T(8,128)}), f32[16,32,128]{2,1,0:T(8,128)S(1)}, u32[]{:S(2)}, u32[]{:S(2)}) %all-to-all-start) | async-done | bytes 262176 | tf_op jit(solution)/shard_map/all_to_all | solution.py:71
  30.4 10.8 %gather_fusion.1 = f32[4096,128]{1,0:T(8,128)S(1)} fusion(f32[512,128]{1,0:T(8,128)S(1)} %bitcast.66, s32[4096]{0:T(1024)S(1)} %broadcast_clamp_fusion), kind=kCustom, calls=%fused_computation.1 | custom fusion | bytes 4210688 | tf_op jit(solution)/shard_map/gather | solution.py:75
  41.1 0.7 fusion.86
  41.8 0.0 copy-start.1
  41.8 0.0 copy-start.3
  41.8 0.7 fusion.87
  42.5 0.5 copy-done.1
  43.0 0.7 copy-done.3
  43.7 3.9 %fusion = (f32[512,128]{1,0:T(8,128)S(1)}, pred[512,8,128]{2,1,0:T(8,128)(4,1)S(1)}, pred[512,8,128]{2,1,0:T(8,128)(4,1)S(1)}, pred[512,8,128]{2,1,0:T(8,128)(4,...) fusion(f32[512,8,126]{2,1,0:T(8,128)S(1)} %get-tuple-element.13, ...), kind=kLoop, calls=%fused_computation.14 | loop fusion | flops 9371648 | bytes 16416768 | tf_op jit(solution)/shard_map/reduce_sum | solution.py:80
  47.7 0.7 slice_bitcast_fusion.1
  48.4 1.3 collective-permute-start
  49.7 4.1 %collective-permute-start.1 = (f32[1,256,128]{2,1,0:T(8,128)}, f32[1,256,128]{2,1,0:T(8,128)}, u32[]{:S(2)}, u32[]{:S(2)}) collective-permute-start(f32[1,256,128]{2,1,0:T(8,128)} %get-tuple-element.33), channel_id=1, source_target_pairs={{0,1},{1,2},{2,3},{3,4},{4,5},{5,6},{6,7},{7,8},{8,9},{9,10},{10,1... | collective-permute-start | bytes 393224 | tf_op jit(solution)/shard_map/ppermute | solution.py:21
  53.8 0.0 copy-start.2
  53.9 0.2 convert_multiply_fusion
  54.1 0.5 copy-done.2
  54.5 2.6 %slice_select_fusion.2 = (f32[512,8,127]{2,1,0:T(8,128)S(1)}, f32[512,8,127]{2,1,0:T(8,128)}) fusion(f32[512,8,128]{2,1,0:T(8,128)S(1)} %convert_multiply_fusion, pred[512,8,128]{2,1,0:T(8,128)(4,1)S(1)} %get-tuple-element.4, pred[512,8,128]{2,1,0:T(8,128)(4,1)S(1)} %get-tuple-element.6), kind=kLoop, calls=%fused_computation.17 | loop fusion | flops 1040384 | bytes 9363456 | tf_op jit(solution)/shard_map/jit(_where)/select_n | solution.py:85
  57.2 3.2 %slice_select_fusion.3 = (f32[512,8,126]{2,1,0:T(8,128)}, f32[512,8,126]{2,1,0:T(8,128)}) fusion(f32[512,8,128]{2,1,0:T(8,128)S(1)} %convert_multiply_fusion, pred[512,8,128]{2,1,0:T(8,128)(4,1)S(1)} %get-tuple-element.3, pred[512,8,128]{2,1,0:T(8,128)(4,1)S(1)} %get-tuple-element.7), kind=kLoop, calls=%fused_computation.18 | loop fusion | flops 1032192 | bytes 9289728 | tf_op jit(solution)/shard_map/jit(_where)/select_n | solution.py:85
  60.3 23.1 %scatter_custom_fusion = f32[512,128]{1,0:T(8,128)} fusion(s32[4096]{0:T(1024)S(1)} %bitcast.75, f32[512,8,126]{2,1,0:T(8,128)} %get-tuple-element.9, f32[]{:T(128)} %constant.10.clone.1, f32[512,8,127]{2,1,0:T(8,128)} %get-tuple-element.11, pred[512,8,128]{2,1,0:T(8,128)(4,1)} %get-tuple-element.5, f32[512,8,127]{2,1,0:T(8,128)S(1)} %get-tuple-element.10, ...), kind=kCustom, calls=%fused_computation.19 | custom fusion | flops 4194304 | bytes 10487296 | tf_op jit(solution)/shard_map/scatter-add | solution.py:89
  83.4 4.6 %all-to-all-start.1 = ((f32[16,32,128]{2,1,0:T(8,128)}), f32[16,32,128]{2,1,0:T(8,128)}, u32[]{:S(2)}, u32[]{:S(2)}) async-start(f32[16,32,128]{2,1,0:T(8,128)} %bitcast.71), calls=%async_computation.1 | async-start | bytes 524288 | tf_op jit(solution)/shard_map/all_to_all | solution.py:92
  88.1 0.0 all-reduce.14.cloned.1.call-start
  88.1 0.0 collective-permute-done
  88.1 0.0 collective-permute-done.1
  88.1 1.2 fusion.90
  89.3 0.0 copy-done.7
  89.3 0.0 copy-start.10
  89.4 0.0 copy-start.6
  89.4 0.2 fusion.56
  89.5 0.1 fusion.89
  89.6 1.3 collective-permute-start.3
  90.9 4.0 %collective-permute-start.5 = (f32[3,1,256,128]{3,2,1,0:T(8,128)S(1)}, f32[3,1,256,128]{3,2,1,0:T(8,128)}, u32[]{:S(2)}, u32[]{:S(2)}) collective-permute-start(f32[3,1,256,128]{3,2,1,0:T(8,128)S(1)} %get-tuple-element.19), channel_id=1, source_target_pairs={{0,1},{1,2},{2,3},{3,4},{4,5},{5,6},{6,7},{7,8},{8,9},{9,10},{10,1... | collective-permute-start | bytes 1179656 | tf_op jit(solution)/shard_map/ppermute | solution.py:21
  94.9 0.0 copy-done.10
  94.9 0.0 collective-permute-done.2
  94.9 0.0 collective-permute-done.4
  94.9 0.0 copy-done.6
  94.9 1.2 fusion.74
  96.1 3.4 %all-to-all-done.1 = f32[16,32,128]{2,1,0:T(8,128)} async-done(((f32[16,32,128]{2,1,0:T(8,128)}), f32[16,32,128]{2,1,0:T(8,128)}, u32[]{:S(2)}, u32[]{:S(2)}) %all-to-all-start.1) | async-done | bytes 262176 | tf_op jit(solution)/shard_map/all_to_all | solution.py:92
  99.6 3.3 %scatter_custom_fusion.1 = f32[512,128]{1,0:T(8,128)} fusion(s32[512]{0:T(512)S(1)} %bitcast.76, f32[512,128]{1,0:T(8,128)} %bitcast.13, f32[]{:T(128)} %constant.10.clone.1), kind=kCustom, calls=%fused_computation.120 | custom fusion | flops 65536 | bytes 262656 | tf_op jit(solution)/shard_map/scatter-add | solution.py:96
  102.9 0.0 all-reduce.14.cloned.1.call-update
  102.9 0.0 collective-permute-done.3
  102.9 0.0 collective-permute-done.5
  102.9 0.0 copy-start
  102.9 1.8 fusion.25
  104.7 0.1 fusion.88
  104.8 1.3 collective-permute-start.6
  106.1 3.9 %collective-permute-start.7 = (f32[3,1,256,128]{3,2,1,0:T(8,128)S(1)}, f32[3,1,256,128]{3,2,1,0:T(8,128)}, u32[]{:S(2)}, u32[]{:S(2)}) collective-permute-start(f32[3,1,256,128]{3,2,1,0:T(8,128)S(1)} %get-tuple-element.17), channel_id=1, source_target_pairs={{0,1},{1,2},{2,3},{3,4},{4,5},{5,6},{6,7},{7,8},{8,9},{9,10},{10,1... | collective-permute-start | bytes 1179656 | tf_op jit(solution)/shard_map/ppermute | solution.py:21
  110.0 85.3 %all-reduce.14.cloned.1.call-done = f32[512,128]{1,0:T(8,128)} async-done(((f32[512,128]{1,0:T(8,128)}), f32[512,128]{1,0:T(8,128)}) %all-reduce.14.cloned.1.call-update) | async-done | bytes 262160 | tf_op jit(solution)/shard_map/psum | solution.py:98
  195.4 1.7 multiply_subtract_fusion
  197.1 0.0 collective-permute-done.6
  197.1 0.0 collective-permute-done.7
  197.1 2.6 %fusion.39 = f32[3,2,256,128]{3,2,1,0:T(8,128)} fusion(f32[3,2,256,128]{3,2,1,0:T(8,128)S(1)} %fusion.25, f32[3,1,256,128]{3,2,1,0:T(8,128)} %collective-permute-done.7, f32[3,1,256,128]{3,2,1,0:T(8,128)} %collective-permute-done.6, f32[2,256,128]{2,1,0:T(8,128)S(1)} %get-tuple-element.22, f32[2,256,128]{2,1,0:T(8,128)S(1)} %get-tuple-element.25, ...), kind=kLoop, calls=%fused_computation.66 | loop fusion | flops 4128768 | bytes 3932160 | tf_op jit(solution)/shard_map/add | solution.py:47
  (14 shorter events, 0.1 us)
Async XLA Ops:
  7.2 18.1 %copy-start.9 = (s32[1,1,16,32]{3,2,1,0:T(8,128)S(1)}, s32[1,1,16,32]{3,2,1,0:T(8,128)}, u32[]{:S(2)}) copy-start(s32[1,1,16,32]{3,2,1,0:T(8,128)} %param.12) | copy-start | bytes 6148
  7.2 12.0 %copy-start.5 = (f32[512,128]{1,0:T(8,128)S(1)}, f32[512,128]{1,0:T(8,128)}, u32[]{:S(2)}) copy-start(f32[512,128]{1,0:T(8,128)} %param.11) | copy-start | bytes 786436
  7.2 17.7 %copy-start.8 = (s32[1,512,8]{1,2,0:T(8,128)S(1)}, s32[1,512,8]{1,2,0:T(8,128)}, u32[]{:S(2)}) copy-start(s32[1,512,8]{1,2,0:T(8,128)} %param.13) | copy-start | bytes 49156
  10.6 19.8 %all-to-all-start = ((f32[16,32,128]{2,1,0:T(8,128)}), f32[16,32,128]{2,1,0:T(8,128)S(1)}, u32[]{:S(2)}, u32[]{:S(2)}) async-start(f32[16,32,128]{2,1,0:T(8,128)} %bitcast.6), calls=%async_computation | async-start | bytes 524288 | tf_op jit(solution)/shard_map/all_to_all | solution.py:71
  19.9 75.0 %collective-permute-start.2 = (f32[1,256,128]{2,1,0:T(8,128)}, f32[1,256,128]{2,1,0:T(8,128)}, u32[]{:S(2)}, u32[]{:S(2)}) collective-permute-start(f32[1,256,128]{2,1,0:T(8,128)} %get-tuple-element.26), channel_id=1, source_target_pairs={{1,0},{2,1},{3,2},{4,3},{5,4},{6,5},{7,6},{8,7},{9,8},{10,9},{11,1... | collective-permute-start | bytes 393224 | tf_op jit(solution)/shard_map/ppermute | solution.py:23
  21.2 73.7 %collective-permute-start.4 = (f32[1,256,128]{2,1,0:T(8,128)}, f32[1,256,128]{2,1,0:T(8,128)}, u32[]{:S(2)}, u32[]{:S(2)}) collective-permute-start(f32[1,256,128]{2,1,0:T(8,128)} %get-tuple-element.27), channel_id=1, source_target_pairs={{0,1},{1,2},{2,3},{3,4},{4,5},{5,6},{6,7},{7,8},{8,9},{9,10},{10,1... | collective-permute-start | bytes 393224 | tf_op jit(solution)/shard_map/ppermute | solution.py:21
  41.8 1.2 copy-start.1
  41.8 1.9 copy-start.3
  43.7 10.1 %copy-start.4 = (f32[1,512,128]{2,1,0:T(8,128)S(1)}, f32[1,512,128]{2,1,0:T(8,128)}, u32[]{:S(2)}) copy-start(f32[1,512,128]{2,1,0:T(8,128)} %param.9) | copy-start | bytes 786436
  48.4 39.7 %collective-permute-start = (f32[1,256,128]{2,1,0:T(8,128)}, f32[1,256,128]{2,1,0:T(8,128)S(1)}, u32[]{:S(2)}, u32[]{:S(2)}) collective-permute-start(f32[1,256,128]{2,1,0:T(8,128)} %get-tuple-element.32), channel_id=1, source_target_pairs={{1,0},{2,1},{3,2},{4,3},{5,4},{6,5},{7,6},{8,7},{9,8},{10,9},{11,1... | collective-permute-start | bytes 393224 | tf_op jit(solution)/shard_map/ppermute | solution.py:23
  49.7 38.4 %collective-permute-start.1 = (f32[1,256,128]{2,1,0:T(8,128)}, f32[1,256,128]{2,1,0:T(8,128)}, u32[]{:S(2)}, u32[]{:S(2)}) collective-permute-start(f32[1,256,128]{2,1,0:T(8,128)} %get-tuple-element.33), channel_id=1, source_target_pairs={{0,1},{1,2},{2,3},{3,4},{4,5},{5,6},{6,7},{7,8},{8,9},{9,10},{10,1... | collective-permute-start | bytes 393224 | tf_op jit(solution)/shard_map/ppermute | solution.py:21
  53.8 0.7 copy-start.2
  83.4 5.9 %copy-start.7 = (f32[1,3,512,128]{3,2,1,0:T(8,128)S(1)}, f32[1,3,512,128]{3,2,1,0:T(8,128)}, u32[]{:S(2)}) copy-start(f32[1,3,512,128]{3,2,1,0:T(8,128)} %param.10) | copy-start | bytes 2359300
  83.4 16.1 %all-to-all-start.1 = ((f32[16,32,128]{2,1,0:T(8,128)}), f32[16,32,128]{2,1,0:T(8,128)}, u32[]{:S(2)}, u32[]{:S(2)}) async-start(f32[16,32,128]{2,1,0:T(8,128)} %bitcast.71), calls=%async_computation.1 | async-start | bytes 524288 | tf_op jit(solution)/shard_map/all_to_all | solution.py:92
  88.1 107.3 %all-reduce.14.cloned.1.call-start = ((), (), s32[]{:S(2)}) async-start(), calls=%async_computation.2 | async-start | bytes 524288 | tf_op jit(solution)/shard_map/psum | solution.py:98
  89.3 5.6 %copy-start.10 = (s32[512,1]{0,1:T(1,128)S(1)}, s32[512,1]{0,1:T(1,128)}, u32[]{:S(2)}) copy-start(s32[512,1]{0,1:T(1,128)} %reshape_squeeze.9) | copy-start | bytes 6148
  89.4 5.6 %copy-start.6 = (f32[512,128]{1,0:T(8,128)S(1)}, f32[512,128]{1,0:T(8,128)}, u32[]{:S(2)}) copy-start(f32[512,128]{1,0:T(8,128)} %param.11) | copy-start | bytes 786436
  89.6 13.3 %collective-permute-start.3 = (f32[3,1,256,128]{3,2,1,0:T(8,128)S(1)}, f32[3,1,256,128]{3,2,1,0:T(8,128)}, u32[]{:S(2)}, u32[]{:S(2)}) collective-permute-start(f32[3,1,256,128]{3,2,1,0:T(8,128)S(1)} %get-tuple-element.18), channel_id=1, source_target_pairs={{1,0},{2,1},{3,2},{4,3},{5,4},{6,5},{7,6},{8,7},{9,8},{10,9},{11,1... | collective-permute-start | bytes 1179656 | tf_op jit(solution)/shard_map/ppermute | solution.py:23
  90.9 12.0 %collective-permute-start.5 = (f32[3,1,256,128]{3,2,1,0:T(8,128)S(1)}, f32[3,1,256,128]{3,2,1,0:T(8,128)}, u32[]{:S(2)}, u32[]{:S(2)}) collective-permute-start(f32[3,1,256,128]{3,2,1,0:T(8,128)S(1)} %get-tuple-element.19), channel_id=1, source_target_pairs={{0,1},{1,2},{2,3},{3,4},{4,5},{5,6},{6,7},{7,8},{8,9},{9,10},{10,1... | collective-permute-start | bytes 1179656 | tf_op jit(solution)/shard_map/ppermute | solution.py:21
  102.9 92.5 %copy-start = (f32[512,128]{1,0:T(8,128)S(1)}, f32[512,128]{1,0:T(8,128)}, u32[]{:S(2)}) copy-start(f32[512,128]{1,0:T(8,128)} %param.8) | copy-start | bytes 786436
  104.8 92.3 %collective-permute-start.6 = (f32[3,1,256,128]{3,2,1,0:T(8,128)S(1)}, f32[3,1,256,128]{3,2,1,0:T(8,128)}, u32[]{:S(2)}, u32[]{:S(2)}) collective-permute-start(f32[3,1,256,128]{3,2,1,0:T(8,128)S(1)} %get-tuple-element.16), channel_id=1, source_target_pairs={{1,0},{2,1},{3,2},{4,3},{5,4},{6,5},{7,6},{8,7},{9,8},{10,9},{11,1... | collective-permute-start | bytes 1179656 | tf_op jit(solution)/shard_map/ppermute | solution.py:23
  106.1 91.0 %collective-permute-start.7 = (f32[3,1,256,128]{3,2,1,0:T(8,128)S(1)}, f32[3,1,256,128]{3,2,1,0:T(8,128)}, u32[]{:S(2)}, u32[]{:S(2)}) collective-permute-start(f32[3,1,256,128]{3,2,1,0:T(8,128)S(1)} %get-tuple-element.17), channel_id=1, source_target_pairs={{0,1},{1,2},{2,3},{3,4},{4,5},{5,6},{6,7},{7,8},{8,9},{9,10},{10,1... | collective-permute-start | bytes 1179656 | tf_op jit(solution)/shard_map/ppermute | solution.py:21
Sparse Core Ops, SparseCore 0:
  103.0 92.3 all-reduce.13
where the time goes:
time: 207 us
  waiting for transfers between devices  93 us (45%)
  other arithmetic  45.8 us (22%)
  starting transfers between devices  34.1 us (16%)
  local copies, waits for them, and re-layouts  19.3 us (9%)
  between operations  14.3 us (7%)
    psum x1, waiting for transfers between devices, per_device(): summed = lax.psum(row_grad, 'subj')  85.3 us
    scatter-add x1, other arithmetic, per_device(): slot_grad = jnp.zeros((slabs * capacity, width), jnp.float32).at[slot_one...  23.1 us
    ppermute x4, starting transfers between devices, extended(): lax.ppermute(tail, axis, [(i, (i + 1) % count) for i in range(ends)])  15.8 us
    gather x1, local copies, waits for them, and re-layouts, per_device(): picked = flat_rows[slot_one]  10.8 us
    all_to_all x1, starting transfers between devices, per_device(): lax.all_to_all(sending, 'slab', split_axis=0, concat_axis=0, tiled=True)  8.57 us
    select_n x2, other arithmetic, per_device(): jnp.where(offset_one == offset, contrib, 0.0)  5.79 us
    ppermute x4, starting transfers between devices, extended(): lax.ppermute(head, axis, [((i + 1) % count, i) for i in range(ends)])  5.14 us
    all_to_all x1, starting transfers between devices, per_device(): lax.all_to_all(slot_grad, 'slab', split_axis=0, concat_axis=0, tiled=True)  4.6 us
  transfers between devices with their start and end apart: 11, of which 3 were waited for; matrix products, arithmetic and copies ran while one was open for 28% of the time, Pallas kernels for 0%

commit v1 on v0

--- a/solution.py
+++ b/solution.py
@@ -95,7 +95,7 @@
         .at[send_one.reshape(-1)]
         .add(returned.reshape(-1, width))
     )
-    summed = lax.psum(row_grad, "subj")
+    summed = jnp.sum(lax.all_gather(row_grad, "subj"), axis=0)
     template_out = template - template_rate * summed / subjects
     warped_grid = warped.reshape(planes, YR, width)
     warped_padded = extended(warped_grid, (("slab", 0),), 1)

time: 207 us -> 161 us (0.78)
  waiting for transfers between devices: 93 us -> 47.2 us
  other arithmetic: 45.8 us -> 42.6 us
  starting transfers between devices: 34.1 us -> 37 us
    psum x1 -> x0, waiting for transfers between devices: 85.3 us -> none  [per_device(): summed = lax.psum(row_grad, 'subj')]
    all_gather x0 -> x1, waiting for transfers between devices: none -> 23.1 us  [per_device(): summed = jnp.sum(lax.all_gather(row_grad, 'subj'), axis=0)]
    all_to_all x1, waiting for transfers between devices: 3.45 us -> 11.2 us  [per_device(): lax.all_to_all(slot_grad, 'slab', split_axis=0, concat_axis=0, tiled=True)]
    all_to_all x1, waiting for transfers between devices: 4.14 us -> 10.5 us  [per_device(): lax.all_to_all(sending, 'slab', split_axis=0, concat_axis=0, tiled=True)]
    ppermute x4, starting transfers between devices: 15.8 us -> 19.6 us  [extended(): lax.ppermute(tail, axis, [(i, (i + 1) % count) for i in range(ends)])]
    reduce_sum x0 -> x1, other arithmetic: none -> 2.44 us  [per_device(): summed = jnp.sum(lax.all_gather(row_grad, 'subj'), axis=0)]
    ppermute x4, waiting for transfers between devices: 0.01 us -> 2.35 us  [extended(): lax.ppermute(tail, axis, [(i, (i + 1) % count) for i in range(ends)])]
    add x2, other arithmetic: 4.45 us -> 2.17 us  [smooth_step(): return center + diffusion_dt * summed]
  transfers between devices with their start and end apart: 11 -> 11, of which waited for: 3 -> 5; matrix products, arithmetic and copies ran while one was open for 28% -> 3% of each run, Pallas kernels for 0% -> 0%
where the time goes in v1:
time: 161 us; the launch traced here: 159 us
  waiting for transfers between devices  47.2 us (29%)
  other arithmetic  42.6 us (26%)
  starting transfers between devices  37 us (23%)
  local copies, waits for them, and re-layouts  18.3 us (11%)
  between operations  14.4 us (9%)
    all_gather x1, waiting for transfers between devices, per_device(): summed = jnp.sum(lax.all_gather(row_grad, 'subj'), axis=0)  23.1 us
    scatter-add x1, other arithmetic, per_device(): slot_grad = jnp.zeros((slabs * capacity, width), jnp.float32).at[slot_one...  23.1 us
    ppermute x4, starting transfers between devices, extended(): lax.ppermute(tail, axis, [(i, (i + 1) % count) for i in range(ends)])  19.6 us
    all_to_all x1, waiting for transfers between devices, per_device(): lax.all_to_all(slot_grad, 'slab', split_axis=0, concat_axis=0, tiled=True)  11.2 us
    gather x1, local copies, waits for them, and re-layouts, per_device(): picked = flat_rows[slot_one]  10.8 us
    all_to_all x1, waiting for transfers between devices, per_device(): lax.all_to_all(sending, 'slab', split_axis=0, concat_axis=0, tiled=True)  10.5 us
    all_to_all x1, starting transfers between devices, per_device(): lax.all_to_all(sending, 'slab', split_axis=0, concat_axis=0, tiled=True)  8.57 us
    select_n x2, other arithmetic, per_device(): jnp.where(offset_one == offset, contrib, 0.0)  5.78 us
  transfers between devices with their start and end apart: 11, of which 5 were waited for; matrix products, arithmetic and copies ran while one was open for 3% of the time, Pallas kernels for 0%

profile of v1, /device:TPU:2, one launch (start us, length us, event | category | flops | bytes accessed | tf_op | source)
XLA Modules:
  0.0 159.5 jit_solution(17962527805601046989)
XLA Ops:
  7.2 0.0 copy-start.8
  7.2 0.7 compare_select_fusion.2
  7.9 0.1 reshape.168
  8.0 2.6 %gather_fusion = f32[512,128]{1,0:T(8,128)} fusion(f32[512,128]{1,0:T(8,128)} %param.8, s32[1024]{0:T(1024)S(1)} %pad_clamp_fusion), kind=kCustom, calls=%fused_computation | custom fusion | bytes 526336 | tf_op jit(solution)/shard_map/gather | solution.py:70
  10.6 8.6 %all-to-all-start = ((f32[16,32,128]{2,1,0:T(8,128)}), f32[16,32,128]{2,1,0:T(8,128)S(1)}, u32[]{:S(2)}, u32[]{:S(2)}) async-start(f32[16,32,128]{2,1,0:T(8,128)} %bitcast.6), calls=%async_computation | async-start | bytes 524288 | tf_op jit(solution)/shard_map/all_to_all | solution.py:71
  19.1 0.0 copy-done.8
  19.1 0.1 copy.12
  19.3 0.2 reshape_squeeze.10
  19.5 0.1 copy.13
  19.6 0.2 reshape.176
  19.8 10.5 %all-to-all-done = f32[16,32,128]{2,1,0:T(8,128)S(1)} async-done(((f32[16,32,128]{2,1,0:T(8,128)}), f32[16,32,128]{2,1,0:T(8,128)S(1)}, u32[]{:S(2)}, u32[]{:S(2)}) %all-to-all-start) | async-done | bytes 262176 | tf_op jit(solution)/shard_map/all_to_all | solution.py:71
  30.3 10.8 %gather_fusion.1 = f32[4096,128]{1,0:T(8,128)S(1)} fusion(f32[512,128]{1,0:T(8,128)S(1)} %bitcast.67, s32[4096]{0:T(1024)S(1)} %broadcast_clamp_fusion), kind=kCustom, calls=%fused_computation.1 | custom fusion | bytes 4210688 | tf_op jit(solution)/shard_map/gather | solution.py:75
  41.1 0.7 fusion.86
  41.8 0.0 copy-start.1
  41.8 0.0 copy-start.3
  41.8 0.7 fusion.87
  42.5 0.5 copy-done.1
  43.0 0.7 copy-done.3
  43.7 3.9 %fusion = (f32[512,128]{1,0:T(8,128)S(1)}, pred[512,8,128]{2,1,0:T(8,128)(4,1)S(1)}, pred[512,8,128]{2,1,0:T(8,128)(4,1)S(1)}, pred[512,8,128]{2,1,0:T(8,128)(4,...) fusion(f32[512,8,126]{2,1,0:T(8,128)S(1)} %get-tuple-element.13, ...), kind=kLoop, calls=%fused_computation.14 | loop fusion | flops 9371648 | bytes 16416768 | tf_op jit(solution)/shard_map/reduce_sum | solution.py:80
  47.6 0.0 copy-done.4
  47.7 0.0 copy-start.2
  47.7 0.2 convert_multiply_fusion
  47.9 0.5 copy-done.2
  48.4 2.6 %slice_select_fusion.2 = (f32[512,8,127]{2,1,0:T(8,128)S(1)}, f32[512,8,127]{2,1,0:T(8,128)}) fusion(f32[512,8,128]{2,1,0:T(8,128)S(1)} %convert_multiply_fusion, pred[512,8,128]{2,1,0:T(8,128)(4,1)S(1)} %get-tuple-element.4, pred[512,8,128]{2,1,0:T(8,128)(4,1)S(1)} %get-tuple-element.6), kind=kLoop, calls=%fused_computation.17 | loop fusion | flops 1040384 | bytes 9363456 | tf_op jit(solution)/shard_map/jit(_where)/select_n | solution.py:85
  51.0 3.2 %slice_select_fusion.3 = (f32[512,8,126]{2,1,0:T(8,128)}, f32[512,8,126]{2,1,0:T(8,128)}) fusion(f32[512,8,128]{2,1,0:T(8,128)S(1)} %convert_multiply_fusion, pred[512,8,128]{2,1,0:T(8,128)(4,1)S(1)} %get-tuple-element.3, pred[512,8,128]{2,1,0:T(8,128)(4,1)S(1)} %get-tuple-element.7), kind=kLoop, calls=%fused_computation.18 | loop fusion | flops 1032192 | bytes 9289728 | tf_op jit(solution)/shard_map/jit(_where)/select_n | solution.py:85
  54.2 23.1 %scatter_custom_fusion = f32[512,128]{1,0:T(8,128)} fusion(s32[4096]{0:T(1024)S(1)} %bitcast.78, f32[512,8,126]{2,1,0:T(8,128)} %get-tuple-element.9, f32[]{:T(128)} %constant.10.clone.1, f32[512,8,127]{2,1,0:T(8,128)} %get-tuple-element.11, pred[512,8,128]{2,1,0:T(8,128)(4,1)} %get-tuple-element.5, f32[512,8,127]{2,1,0:T(8,128)S(1)} %get-tuple-element.10, ...), kind=kCustom, calls=%fused_computation.19 | custom fusion | flops 4194304 | bytes 10487296 | tf_op jit(solution)/shard_map/scatter-add | solution.py:89
  77.2 3.7 %all-to-all-start.1 = ((f32[16,32,128]{2,1,0:T(8,128)}), f32[16,32,128]{2,1,0:T(8,128)S(1)}, u32[]{:S(2)}, u32[]{:S(2)}) async-start(f32[16,32,128]{2,1,0:T(8,128)} %bitcast.73), calls=%async_computation.1 | async-start | bytes 524288 | tf_op jit(solution)/shard_map/all_to_all | solution.py:92
  80.9 0.0 all-gather.3.cloned.1.call-start
  81.0 0.0 copy-done.9
  81.0 0.1 reshape_squeeze.9
  81.1 11.2 %all-to-all-done.1 = f32[16,32,128]{2,1,0:T(8,128)S(1)} async-done(((f32[16,32,128]{2,1,0:T(8,128)}), f32[16,32,128]{2,1,0:T(8,128)S(1)}, u32[]{:S(2)}, u32[]{:S(2)}) %all-to-all-start.1) | async-done | bytes 262176 | tf_op jit(solution)/shard_map/all_to_all | solution.py:92
  92.2 2.9 %scatter_custom_fusion.1 = f32[512,128]{1,0:T(8,128)} fusion(s32[512]{0:T(512)S(1)} %bitcast.79, f32[512,128]{1,0:T(8,128)S(1)} %bitcast.77, f32[]{:T(128)} %constant.10.clone.1), kind=kCustom, calls=%fused_computation.120 | custom fusion | flops 65536 | bytes 262148 | tf_op jit(solution)/shard_map/scatter-add | solution.py:96
  95.2 0.0 all-gather.3.cloned.1.call-update
  95.2 1.3 collective-permute-start
  96.5 3.2 %collective-permute-start.1 = (f32[1,256,128]{2,1,0:T(8,128)S(1)}, f32[1,256,128]{2,1,0:T(8,128)S(1)}, u32[]{:S(2)}, u32[]{:S(2)}) collective-permute-start(f32[1,256,128]{2,1,0:T(8,128)S(1)} %get-tuple-element.33), channel_id=1, source_target_pairs={{0,1},{1,2},{2,3},{3,4},{4,5},{5,6},{6,7},{7,8},{8,9},{9,10},{10,1... | collective-permute-start | bytes 393224 | tf_op jit(solution)/shard_map/ppermute | solution.py:21
  99.7 1.0 slice_bitcast_fusion.3
  100.7 1.3 collective-permute-start.2
  102.0 4.5 %collective-permute-start.4 = (f32[1,256,128]{2,1,0:T(8,128)S(1)}, f32[1,256,128]{2,1,0:T(8,128)S(1)}, u32[]{:S(2)}, u32[]{:S(2)}) collective-permute-start(f32[1,256,128]{2,1,0:T(8,128)S(1)} %get-tuple-element.27), channel_id=1, source_target_pairs={{0,1},{1,2},{2,3},{3,4},{4,5},{5,6},{6,7},{7,8},{8,9},{9,10},{10,1... | collective-permute-start | bytes 393224 | tf_op jit(solution)/shard_map/ppermute | solution.py:21
  106.4 0.0 collective-permute-done
  106.5 0.0 collective-permute-done.1
  106.5 0.0 copy-done.5
  106.5 0.2 fusion.90
  106.7 0.0 copy-done.7
  106.7 0.0 copy-start.6
  106.7 0.2 fusion.56
  106.9 0.1 fusion.89
  106.9 1.3 collective-permute-start.3
  108.2 4.3 %collective-permute-start.5 = (f32[3,1,256,128]{3,2,1,0:T(8,128)S(1)}, f32[3,1,256,128]{3,2,1,0:T(8,128)S(1)}, u32[]{:S(2)}, u32[]{:S(2)}) collective-permute-start(f32[3,1,256,128]{3,2,1,0:T(8,128)S(1)} %get-tuple-element.19), channel_id=1, source_target_pairs={{0,1},{1,2},{2,3},{3,4},{4,5},{5,6},{6,7},{7,8},{8,9},{9,10},{10,1... | collective-permute-start | bytes 1179656 | tf_op jit(solution)/shard_map/ppermute | solution.py:21
  112.5 0.0 collective-permute-done.2
  112.5 0.0 collective-permute-done.4
  112.6 0.0 copy-done.6
  112.6 0.2 fusion.74
  112.8 0.0 collective-permute-done.3
  112.8 1.0 collective-permute-done.5
  113.8 0.6 fusion.25
  114.5 0.1 fusion.88
  114.6 1.3 collective-permute-start.6
  115.9 7.7 %collective-permute-start.7 = (f32[3,1,256,128]{3,2,1,0:T(8,128)S(1)}, f32[3,1,256,128]{3,2,1,0:T(8,128)S(1)}, u32[]{:S(2)}, u32[]{:S(2)}) collective-permute-start(f32[3,1,256,128]{3,2,1,0:T(8,128)S(1)} %get-tuple-element.17), channel_id=1, source_target_pairs={{0,1},{1,2},{2,3},{3,4},{4,5},{5,6},{6,7},{7,8},{8,9},{9,10},{10,1... | collective-permute-start | bytes 1179656 | tf_op jit(solution)/shard_map/ppermute | solution.py:21
  123.5 0.0 collective-permute-done.6
  123.5 1.3 collective-permute-done.7
  124.8 1.5 fusion.39
  126.4 23.1 %all-gather.3.cloned.1.call-done = f32[8192,128]{1,0:T(8,128)} async-done(((f32[512,128]{1,0:T(8,128)}), f32[8192,128]{1,0:T(8,128)}) %all-gather.3.cloned.1.call-update) | async-done | bytes 4194320 | tf_op jit(solution)/shard_map/all_gather | solution.py:98
  149.5 2.4 %reduce_sum.21 = f32[512,128]{1,0:T(8,128)S(1)} reduce(f32[16,512,128]{2,1,0:T(8,128)} %bitcast.71, f32[]{:T(128)} %constant.10.clone.1), dimensions={0}, to_apply=%region_3.4 | reduce | flops 983040 | bytes 4456452 | tf_op jit(solution)/shard_map/reduce_sum | solution.py:98
  151.9 0.7 multiply_subtract_fusion
  (13 shorter events, 0.1 us)
Async XLA Ops:
  7.2 12.0 %copy-start.8 = (s32[1,512,8]{1,2,0:T(8,128)S(1)}, s32[1,512,8]{1,2,0:T(8,128)}, u32[]{:S(2)}) copy-start(s32[1,512,8]{1,2,0:T(8,128)} %param.13) | copy-start | bytes 49156
  10.6 19.8 %all-to-all-start = ((f32[16,32,128]{2,1,0:T(8,128)}), f32[16,32,128]{2,1,0:T(8,128)S(1)}, u32[]{:S(2)}, u32[]{:S(2)}) async-start(f32[16,32,128]{2,1,0:T(8,128)} %bitcast.6), calls=%async_computation | async-start | bytes 524288 | tf_op jit(solution)/shard_map/all_to_all | solution.py:71
  41.8 1.2 copy-start.1
  41.8 1.9 %copy-start.3 = (s32[1,512,8,128]{3,2,1,0:T(8,128)S(1)}, s32[1,512,8,128]{3,2,1,0:T(8,128)}, u32[]{:S(2)}) copy-start(s32[1,512,8,128]{3,2,1,0:T(8,128)} %param.14) | copy-start | bytes 6291460
  43.7 3.9 %copy-start.4 = (f32[1,512,128]{2,1,0:T(8,128)S(1)}, f32[1,512,128]{2,1,0:T(8,128)}, u32[]{:S(2)}) copy-start(f32[1,512,128]{2,1,0:T(8,128)} %param.9) | copy-start | bytes 786436
  47.7 0.7 copy-start.2
  54.2 26.8 %copy-start.9 = (s32[1,1,16,32]{3,2,1,0:T(8,128)S(1)}, s32[1,1,16,32]{3,2,1,0:T(8,128)}, u32[]{:S(2)}) copy-start(s32[1,1,16,32]{3,2,1,0:T(8,128)} %param.12) | copy-start | bytes 6148
  77.2 29.2 %copy-start.5 = (f32[1,512,128]{2,1,0:T(8,128)S(1)}, f32[1,512,128]{2,1,0:T(8,128)}, u32[]{:S(2)}) copy-start(f32[1,512,128]{2,1,0:T(8,128)} %param.9) | copy-start | bytes 786436
  77.2 29.5 %copy-start.7 = (f32[1,3,512,128]{3,2,1,0:T(8,128)S(1)}, f32[1,3,512,128]{3,2,1,0:T(8,128)}, u32[]{:S(2)}) copy-start(f32[1,3,512,128]{3,2,1,0:T(8,128)} %param.10) | copy-start | bytes 2359300
  77.2 15.0 %all-to-all-start.1 = ((f32[16,32,128]{2,1,0:T(8,128)}), f32[16,32,128]{2,1,0:T(8,128)S(1)}, u32[]{:S(2)}, u32[]{:S(2)}) async-start(f32[16,32,128]{2,1,0:T(8,128)} %bitcast.73), calls=%async_computation.1 | async-start | bytes 524288 | tf_op jit(solution)/shard_map/all_to_all | solution.py:92
  80.9 68.5 %all-gather.3.cloned.1.call-start = ((), (), s32[]{:S(2)}) async-start(), calls=%async_computation.2 | async-start | bytes 4456448 | tf_op jit(solution)/shard_map/all_gather | solution.py:98
  95.2 11.2 %collective-permute-start = (f32[1,256,128]{2,1,0:T(8,128)S(1)}, f32[1,256,128]{2,1,0:T(8,128)S(1)}, u32[]{:S(2)}, u32[]{:S(2)}) collective-permute-start(f32[1,256,128]{2,1,0:T(8,128)S(1)} %get-tuple-element.32), channel_id=1, source_target_pairs={{1,0},{2,1},{3,2},{4,3},{5,4},{6,5},{7,6},{8,7},{9,8},{10,9},{11,1... | collective-permute-start | bytes 393224 | tf_op jit(solution)/shard_map/ppermute | solution.py:23
  96.5 9.9 %collective-permute-start.1 = (f32[1,256,128]{2,1,0:T(8,128)S(1)}, f32[1,256,128]{2,1,0:T(8,128)S(1)}, u32[]{:S(2)}, u32[]{:S(2)}) collective-permute-start(f32[1,256,128]{2,1,0:T(8,128)S(1)} %get-tuple-element.33), channel_id=1, source_target_pairs={{0,1},{1,2},{2,3},{3,4},{4,5},{5,6},{6,7},{7,8},{8,9},{9,10},{10,1... | collective-permute-start | bytes 393224 | tf_op jit(solution)/shard_map/ppermute | solution.py:21
  100.7 11.8 %collective-permute-start.2 = (f32[1,256,128]{2,1,0:T(8,128)S(1)}, f32[1,256,128]{2,1,0:T(8,128)S(1)}, u32[]{:S(2)}, u32[]{:S(2)}) collective-permute-start(f32[1,256,128]{2,1,0:T(8,128)S(1)} %get-tuple-element.26), channel_id=1, source_target_pairs={{1,0},{2,1},{3,2},{4,3},{5,4},{6,5},{7,6},{8,7},{9,8},{10,9},{11,1... | collective-permute-start | bytes 393224 | tf_op jit(solution)/shard_map/ppermute | solution.py:23
  102.0 10.6 %collective-permute-start.4 = (f32[1,256,128]{2,1,0:T(8,128)S(1)}, f32[1,256,128]{2,1,0:T(8,128)S(1)}, u32[]{:S(2)}, u32[]{:S(2)}) collective-permute-start(f32[1,256,128]{2,1,0:T(8,128)S(1)} %get-tuple-element.27), channel_id=1, source_target_pairs={{0,1},{1,2},{2,3},{3,4},{4,5},{5,6},{6,7},{7,8},{8,9},{9,10},{10,1... | collective-permute-start | bytes 393224 | tf_op jit(solution)/shard_map/ppermute | solution.py:21
  106.7 5.8 %copy-start.6 = (f32[512,128]{1,0:T(8,128)S(1)}, f32[512,128]{1,0:T(8,128)}, u32[]{:S(2)}) copy-start(f32[512,128]{1,0:T(8,128)} %param.11) | copy-start | bytes 786436
  106.9 5.8 %collective-permute-start.3 = (f32[3,1,256,128]{3,2,1,0:T(8,128)S(1)}, f32[3,1,256,128]{3,2,1,0:T(8,128)S(1)}, u32[]{:S(2)}, u32[]{:S(2)}) collective-permute-start(f32[3,1,256,128]{3,2,1,0:T(8,128)S(1)} %get-tuple-element.18), channel_id=1, source_target_pairs={{1,0},{2,1},{3,2},{4,3},{5,4},{6,5},{7,6},{8,7},{9,8},{10,9},{11,1... | collective-permute-start | bytes 1179656 | tf_op jit(solution)/shard_map/ppermute | solution.py:23
  108.2 5.6 %collective-permute-start.5 = (f32[3,1,256,128]{3,2,1,0:T(8,128)S(1)}, f32[3,1,256,128]{3,2,1,0:T(8,128)S(1)}, u32[]{:S(2)}, u32[]{:S(2)}) collective-permute-start(f32[3,1,256,128]{3,2,1,0:T(8,128)S(1)} %get-tuple-element.19), channel_id=1, source_target_pairs={{0,1},{1,2},{2,3},{3,4},{4,5},{5,6},{6,7},{7,8},{8,9},{9,10},{10,1... | collective-permute-start | bytes 1179656 | tf_op jit(solution)/shard_map/ppermute | solution.py:21
  114.6 9.0 %collective-permute-start.6 = (f32[3,1,256,128]{3,2,1,0:T(8,128)S(1)}, f32[3,1,256,128]{3,2,1,0:T(8,128)S(1)}, u32[]{:S(2)}, u32[]{:S(2)}) collective-permute-start(f32[3,1,256,128]{3,2,1,0:T(8,128)S(1)} %get-tuple-element.16), channel_id=1, source_target_pairs={{1,0},{2,1},{3,2},{4,3},{5,4},{6,5},{7,6},{8,7},{9,8},{10,9},{11,1... | collective-permute-start | bytes 1179656 | tf_op jit(solution)/shard_map/ppermute | solution.py:23
  115.9 9.0 %collective-permute-start.7 = (f32[3,1,256,128]{3,2,1,0:T(8,128)S(1)}, f32[3,1,256,128]{3,2,1,0:T(8,128)S(1)}, u32[]{:S(2)}, u32[]{:S(2)}) collective-permute-start(f32[3,1,256,128]{3,2,1,0:T(8,128)S(1)} %get-tuple-element.17), channel_id=1, source_target_pairs={{0,1},{1,2},{2,3},{3,4},{4,5},{5,6},{6,7},{7,8},{8,9},{9,10},{10,1... | collective-permute-start | bytes 1179656 | tf_op jit(solution)/shard_map/ppermute | solution.py:21
  149.5 2.5 %copy-start = (f32[512,128]{1,0:T(8,128)S(1)}, f32[512,128]{1,0:T(8,128)}, u32[]{:S(2)}) copy-start(f32[512,128]{1,0:T(8,128)} %param.8) | copy-start | bytes 786436
Sparse Core Ops, SparseCore 0:
  95.3 54.1 all-gather.2
